TPU v7x, 32 devices: a whole 2x2x4 slice. The times are simulated.
32 devices in a mesh: gx: 8 (over y, x, core), gy: 4 (over z).
Axes of the slice: x: 2, y: 2, z: 4, core: 2. Of those that a mesh axis runs over, the one named last changes fastest.
Arguments:
- populations: float32 [19, 64, 64, 128], P(None, 'gx', 'gy')
- anchor: int32 [8, 4, 1024], P('gx', 'gy'), may hold values from 0 to 20606, as said below
- offsets: float32 [8, 4, 3, 1024], P('gx', 'gy'), may hold values from 0 to 0.999
- heading: float32 [8, 4, 2, 1024], P('gx', 'gy'), may hold values from -3.140625 to 3.140625
- velocity: float32 [8, 4, 3, 1024], P('gx', 'gy'), may hold values from -0.6 to 0.6
- live_count: int32 [8, 4], P('gx', 'gy'), may hold values from 1 to 1024, as said below
Outputs:
- populations_next: float32 [19, 64, 64, 128], P(None, 'gx', 'gy')
- swimmer_force: float32 [8, 4, 3, 1024], P('gx', 'gy')
Inputs may be any that keep to these rules, and one draw needn't show every extreme that they name: The anchor is (ax (18) + ay) * 128 + az with 0 <= ax <= 8, 0 <= ay <= 16, 0 <= az <= 126. Live swimmers fill slots 0 to live_count - 1 of their device; some device holds 1024.
All inputs are finite; a program needn't handle non-finite values.
Results may differ from a plain program's by a relative error of at most 0.0003.
Values sent between devices are 32-bit elements; how exact they have to be, the bound alone decides.
No kernel may reach another device: no remote copies, remote signals or barrier semaphores. Data moves between devices by JAX's collectives and lax.ppermute only.
A program may use at most 64 MiB of HBM per device.

v0:
```python
import functools

import jax
import jax.numpy as jnp
from jax import lax
from jax.experimental import pallas as pl
from jax.experimental.pallas import tpu as pltpu
from jax.sharding import PartitionSpec as P

lattice_dirs = (
    (0, 0, 0),
    (1, 0, 0),
    (-1, 0, 0),
    (0, 1, 0),
    (0, -1, 0),
    (0, 0, 1),
    (0, 0, -1),
    (1, 1, 0),
    (-1, -1, 0),
    (1, -1, 0),
    (-1, 1, 0),
    (1, 0, 1),
    (-1, 0, -1),
    (1, 0, -1),
    (-1, 0, 1),
    (0, 1, 1),
    (0, -1, -1),
    (0, 1, -1),
    (0, -1, 1),
)
lattice_weights = (1.0 / 3.0,) + (1.0 / 18.0,) * 6 + (1.0 / 36.0,) * 12
relax_time = 0.8
friction = 2.0
propulsion = 0.5
wca_energy = 0.01
floor_square = 0.8
cutoff_square = 2.0 ** (1.0 / 3.0)

f32 = jnp.float32
bf16 = jnp.bfloat16
LANES = 128
SUB = 8
FAR = 1.0e9
YPAD = 24
STRIP = 12


def outward(axis, sign):
    return [q for q in range(19) if lattice_dirs[q][axis] == sign]


def split(value):
    high = value.astype(bf16)
    low = (value - high.astype(f32)).astype(bf16)
    return high, low


REACH = 1.1225


def moments_into(pops, mom):
    rho = pops[0]
    for q in range(1, 19):
        rho = rho + pops[q]
    inverse = 1.0 / rho
    mom[3] = rho
    for c in range(3):
        total = None
        for q in range(19):
            sign = lattice_dirs[q][c]
            if sign == 0:
                continue
            term = pops[q] if sign == 1 else -pops[q]
            total = term if total is None else total + term
        mom[c] = total * inverse


def thirds(fields):
    first = fields.astype(bf16).astype(f32)
    second = (fields - first).astype(bf16).astype(f32)
    third = fields - first - second
    return jnp.concatenate([first, second, third, jnp.zeros_like(first)], axis=0).astype(bf16)


def ranks_of(mask, chunks):
    rows = mask.shape[0]
    i = lax.broadcasted_iota(jnp.int32, (LANES, LANES), 0)
    j = lax.broadcasted_iota(jnp.int32, (LANES, LANES), 1)
    upper = jnp.where(i <= j, 1.0, 0.0).astype(bf16)
    ones = jnp.ones((LANES, LANES), bf16)
    held = mask.astype(bf16)
    inside = jnp.dot(held, upper, preferred_element_type=f32)
    total = jnp.dot(held, ones, preferred_element_type=f32)
    i = lax.broadcasted_iota(jnp.int32, (rows, rows), 0)
    j = lax.broadcasted_iota(jnp.int32, (rows, rows), 1)
    ahead = (i > j) & (lax.div(i, chunks) == lax.div(j, chunks))
    before = jnp.dot(jnp.where(ahead, 1.0, 0.0).astype(bf16), total.astype(bf16), preferred_element_type=f32)
    return jnp.where(mask > 0.5, inside + before - 1.0, -1.0)


def chunks_of(count):
    return lax.div(count + (LANES - 1), LANES)


UNROLL = 2


def steps_of(count):
    return lax.div(count + (UNROLL * LANES - 1), UNROLL * LANES)


def compact_into(put, parts, rank, count, chunks):
    def step(j, carry):
        rows = lax.broadcasted_iota(jnp.int32, (LANES, LANES), 0).astype(f32) + (j * LANES).astype(f32)
        chosen = [jnp.where(rows == rank[k : k + 1], 1.0, 0.0).astype(bf16) for k in range(chunks)]
        got = lax.dot_general(
            parts, jnp.concatenate(chosen, axis=1), (((1,), (1,)), ((), ())), preferred_element_type=f32
        )
        tile = got[0:8] + got[8:16] + got[16:24]
        row = lax.broadcasted_iota(jnp.int32, (SUB, LANES), 0)
        tile = jnp.where((row == 0) & (tile[6:7] < 0.5), FAR, tile)
        tile = jnp.where(row == 7, count.astype(f32), tile)
        put(j, tile)
        return carry

    step(jnp.int32(0), 0)
    lax.fori_loop(1, chunks_of(count), step, 0)


def views(mix, cx, cy, nz, chunks):
    rows = 4 * cx * cy
    mom = mix.at[0:rows].reshape(4, cx, cy, nz)
    own = mix.at[rows : rows + SUB * chunks].reshape(chunks, SUB, LANES)
    ranks = mix.at[rows + SUB * chunks : rows + (SUB + 4) * chunks]
    rows = rows + (SUB + 4) * chunks
    return mom, own, ranks, mix.at[rows : rows + 10 * cy].reshape(10, cy, nz)


def pack_y(pops_in, anchor_in, offsets_in, heading_in, velocity_in, count, mix, up, down,
           pops, anchor, offsets, heading, velocity, angles, sems, *, cx, cy, nz, slots):
    chunks = slots // LANES
    mom, own, ranks, faces = views(mix, cx, cy, nz, chunks)
    copies = [
        pltpu.make_async_copy(source, target, sems.at[n])
        for n, (source, target) in enumerate(
            ((anchor_in, anchor), (offsets_in, offsets), (heading_in, heading), (velocity_in, velocity), (pops_in, pops))
        )
    ]
    for copy in copies:
        copy.start()
    for copy in copies[:4]:
        copy.wait()
    number = anchor[...].astype(f32)
    block_row = (cy + 2) * nz
    cell_x = jnp.floor((number + 0.5) * (1.0 / block_row))
    rest = number - cell_x * block_row
    cell_y = jnp.floor((rest + 0.5) * (1.0 / nz))
    cell_z = rest - cell_y * nz
    slot = lax.broadcasted_iota(jnp.int32, (chunks, LANES), 0) * LANES
    live = slot + lax.broadcasted_iota(jnp.int32, (chunks, LANES), 1) < count[0, 0]
    for n in range(2):
        for k in range(chunks):
            angles[n, k : k + 1, :] = heading[n : n + 1, k * LANES : (k + 1) * LANES]
    cosine = jnp.cos(angles[...])
    sine = jnp.sin(angles[...])
    alive = live.astype(f32)
    place_x = jnp.where(live, cell_x - 1.0 + offsets[0:chunks, :], FAR)
    place_y = cell_y - 1.0 + offsets[chunks : 2 * chunks, :]
    rows = [
        place_x,
        place_y,
        cell_z + offsets[2 * chunks : 3 * chunks, :],
        friction * velocity[0:chunks, :] - propulsion * cosine[0] * cosine[1],
        friction * velocity[chunks : 2 * chunks, :] - propulsion * sine[0] * cosine[1],
        friction * velocity[2 * chunks : 3 * chunks, :] - propulsion * sine[1],
        alive,
        jnp.full((chunks, LANES), count[0, 0].astype(f32)),
    ]
    for f in range(8):
        own[:, f, :] = rows[f]
    masks = [
        jnp.where(place_y > cy - 1 - REACH, alive, 0.0),
        jnp.where(place_y < REACH, alive, 0.0),
        jnp.where(place_x > cx - 1 - REACH, alive, 0.0),
        jnp.where(place_x < REACH, alive, 0.0),
    ]
    place = ranks_of(jnp.concatenate(masks, axis=0), chunks)
    ranks[...] = place
    parts = thirds(jnp.concatenate([own[k] for k in range(chunks)], axis=1))
    for n, ref in ((0, up), (1, down)):
        rank = place[n * chunks : (n + 1) * chunks]
        total = jnp.max(rank).astype(jnp.int32) + 1

        def put(j, tile, ref=ref):
            ref[STRIP + j] = tile

        compact_into(put, parts, rank, total, chunks)

    copies[4].wait()
    moments_into(pops, mom)
    for side, sign, ring in ((0, 1, cx - 1), (1, -1, 0)):
        for k, q in enumerate(outward(0, sign)):
            faces[5 * side + k] = pops[q, ring]
    for ref, rows, sign in ((up, (cy - 2, cy - 1), 1), (down, (0, 1), -1)):
        ring = cy - 1 if sign == 1 else 0
        for c in range(3):
            for k in range(2):
                ref[2 * c + k] = mom[c, :, rows[k], :]
        ref[6] = mom[3, :, ring, :]
        for k, q in enumerate(outward(1, sign)):
            ref[7 + k] = pops[q, :, ring, :]


def tent(length, first, place):
    cell = jnp.floor(place)
    part = place - cell
    rows = lax.broadcasted_iota(jnp.int32, (length, LANES), 0).astype(f32) + first
    return jnp.where(rows == cell, 1.0 - part, jnp.where(rows == cell + 1.0, part, 0.0))


def both(value, rows, padded=None):
    value = value.reshape(rows, LANES)
    if padded is not None:
        value = jnp.concatenate([value, jnp.zeros((padded - rows, LANES), f32)], axis=0)
    high, low = split(value)
    return jnp.concatenate([high, low], axis=1)


def along_z(tile, nz):
    high, low = split(tent(nz, 0.0, tile[2:3]))
    return high, low


def sample_table(high, low):
    top = jnp.concatenate([high, low], axis=1)
    return jnp.concatenate([top, top], axis=0)


def gather_rows(table, right):
    full = jnp.dot(table, right, preferred_element_type=f32)
    return full[:, :LANES] + full[:, LANES:]


def spread_many(lefts, highs, lows):
    tall = jnp.concatenate([jnp.concatenate(highs, axis=1), jnp.concatenate(lows, axis=1)], axis=0)
    left = jnp.concatenate(lefts, axis=1)
    full = lax.dot_general(left, tall, (((1,), (1,)), ((), ())), preferred_element_type=f32)
    return full[:, :LANES] + full[:, LANES:]


def spread_rows(left, high, low):
    return spread_many([left], [high, high], [low, low])


def own_first(mix, part, sides, table, *, cx, cy, nz, slots):
    chunks = slots // LANES
    mom, own, ranks, _ = views(mix, cx, cy, nz, chunks)
    fields = jnp.concatenate([own[k] for k in range(chunks)], axis=1)
    parts = thirds(fields)
    for n in range(2):
        rank = ranks[(2 + n) * chunks : (3 + n) * chunks, :]
        total = jnp.max(rank).astype(jnp.int32) + 1

        def put(j, tile, n=n):
            sides[n, j] = tile

        compact_into(put, parts, rank, total, chunks)
    for c in range(3):
        table[c * cx * cy : (c + 1) * cx * cy, :] = both(mom[c], cx * cy)

    def step(n, carry):
        for k in [n * UNROLL + u for u in range(UNROLL)]:
            tile = own[k]
            right = sample_table(*along_z(tile, nz))
            wx = tent(cx, 0.0, tile[0:1])
            wy = tent(cy, 0.0, tile[1:2])
            sums = []
            for c in range(3):
                full = gather_rows(table[c * cx * cy : (c + 1) * cx * cy, :], right).reshape(cx, cy, LANES)
                total = full[0] * wx[0:1]
                for x in range(1, cx):
                    total = total + full[x] * wx[x : x + 1]
                sums.append(jnp.sum(total * wy, axis=0, keepdims=True))
            part[k, 0:3, :] = jnp.concatenate(sums, axis=0)
        return carry

    count = jnp.max(own[0, 7:8, :]).astype(jnp.int32)
    lax.fori_loop(0, steps_of(count), step, 0)


def pack_x(mix, sides, from_down, from_up, right, left, *, cx, cy, nz, slots):
    chunks = slots // LANES
    mom, _, _, faces = views(mix, cx, cy, nz, chunks)
    for side, ref, cols, sign in ((0, right, (cx - 2, cx - 1), 1), (1, left, (0, 1), -1)):
        ring = cx - 1 if sign == 1 else 0
        names = outward(0, sign)
        zero = jnp.zeros((YPAD, LANES), f32)
        for f in range(STRIP):
            ref[f] = zero
        for c in range(3):
            for k in range(2):
                ref[2 * c + k, 2 : 2 + cy, :] = mom[c, cols[k]]
                ref[2 * c + k, 0:2, :] = from_down[2 * c : 2 * c + 2, cols[k], :]
                ref[2 * c + k, 2 + cy : 4 + cy, :] = from_up[2 * c : 2 * c + 2, cols[k], :]
        ref[6, 2 : 2 + cy, :] = mom[3, ring]
        ref[6, 1:2, :] = from_down[6, ring : ring + 1, :]
        ref[6, 2 + cy : 3 + cy, :] = from_up[6, ring : ring + 1, :]
        for k, q in enumerate(names):
            ref[7 + k, 2 : 2 + cy, :] = faces[5 * side + k]
            if lattice_dirs[q][1] == 1:
                at = 7 + outward(1, 1).index(q)
                ref[7 + k, 1:2, :] = from_down[at, ring : ring + 1, :]
            if lattice_dirs[q][1] == -1:
                at = 7 + outward(1, -1).index(q)
                ref[7 + k, 2 + cy : 3 + cy, :] = from_up[at, ring : ring + 1, :]
        for part in range(3):
            for k in range(chunks):
                tile = (sides[side, k], from_down[STRIP + k], from_up[STRIP + k])[part]
                ref[STRIP + part * (chunks // 3 + 1) + k // 3, (k % 3) * SUB : (k % 3 + 1) * SUB, :] = tile


def ghost_rows(gb, tile, at, shift_x, shift_y, nz):
    flat = jnp.transpose(tile)
    rows = pl.ds(pl.multiple_of(at, SUB), LANES)
    gb[0, rows, :] = jnp.broadcast_to(flat[:, 0:1] + shift_x, (LANES, LANES))
    gb[1, rows, :] = jnp.broadcast_to(flat[:, 1:2] + shift_y, (LANES, LANES))
    gb[2, rows, :] = jnp.broadcast_to(flat[:, 2:3] * (1.0 / nz), (LANES, LANES))


GROUP = 16


def pair_rows(gb, tile, rows, total, nz):
    px, py = (jnp.broadcast_to(tile[c : c + 1], (SUB, LANES)) for c in range(2))
    pz = jnp.broadcast_to(tile[2:3] * (1.0 / nz), (SUB, LANES))

    def step(g, total):
        fx, fy, fz = total
        for r in range(GROUP):
            at = pl.ds(pl.multiple_of((g * GROUP + r) * SUB, SUB), SUB)
            dx = px - gb[0, at, :]
            dy = py - gb[1, at, :]
            dz = pz - gb[2, at, :]
            dz = (dz - jnp.round(dz)) * float(nz)
            raw = dx * dx + dy * dy + dz * dz
            square = jnp.maximum(raw, floor_square)
            inverse = pl.reciprocal(square, approx=True)
            inverse = inverse * (2.0 - square * inverse)
            sixth = inverse * inverse * inverse
            size = (sixth * (sixth - 0.5)) * inverse
            size = jnp.where(raw < cutoff_square, size, 0.0)
            fx = fx + size * dx
            fy = fy + size * dy
            fz = fz + size * dz
        return fx, fy, fz

    return lax.fori_loop(0, rows, step, total)


def own_second(mix, part, from_down, from_up, spread_out, react_out, pairs, gb, ytable, *, cx, cy, nz, slots):
    chunks = slots // LANES
    _, own, _, _ = views(mix, cx, cy, nz, chunks)
    count = jnp.max(own[0, 7:8, :]).astype(jnp.int32)
    live_chunks = chunks_of(count)
    wide = cx + 2
    ring = jnp.concatenate(
        [from_down[2 * c + 1] for c in range(3)] + [from_up[2 * c] for c in range(3)], axis=0
    )
    ytable[...] = both(ring, 6 * cx)
    spread_out[...] = jnp.zeros_like(spread_out)

    def step(n, carry):
        lefts, highs, lows = [], [], []
        for k in [n * UNROLL + u for u in range(UNROLL)]:
            tile = own[k]
            high, low = along_z(tile, nz)
            wx = tent(wide + 6, -1.0, tile[0:1])
            wy = tent(YPAD, -2.0, tile[1:2])
            full = gather_rows(ytable[...], sample_table(high, low)).reshape(2, 3, cx, LANES)
            inner = tent(cx, 0.0, tile[0:1])
            lower = jnp.sum(full[0] * inner[None], axis=1) * wy[1:2]
            upper = jnp.sum(full[1] * inner[None], axis=1) * wy[cy + 2 : cy + 3]
            react = tile[3:6] - friction * (part[k, 0:3, :] + lower + upper)
            react_out[k, 0:3, :] = react
            react = react * tile[6:7]
            pieces = []
            for x in range(wide):
                for c in range(3):
                    pieces.append((wx[x : x + 1] * react[c : c + 1]) * wy)
            lefts.append(both(jnp.stack(pieces), wide * 3 * YPAD))
            highs += [high, high]
            lows += [low, low]
        spread_out[...] += spread_many(lefts, highs, lows).reshape(wide, 3, YPAD, LANES)
        return carry

    lax.fori_loop(0, steps_of(count), step, 0)

    pairs[...] = jnp.zeros_like(pairs)

    def fill(k, carry):
        ghost_rows(gb, own[k], k * LANES, 0.0, 0.0, nz)
        return carry

    lax.fori_loop(0, live_chunks, fill, 0)
    groups = lax.div(count + (GROUP * SUB - 1), GROUP * SUB)

    def own_step(k, carry):
        zero = jnp.zeros((SUB, LANES), f32)
        total = pair_rows(gb, own[k], groups, (zero, zero, zero), nz)
        for c in range(3):
            pairs[k, c] = total[c]
        return carry

    lax.fori_loop(0, live_chunks, own_step, 0)


def post_of(q, pop, rho, u, force, common):
    c = lattice_dirs[q]
    w = lattice_weights[q]

    def dot(v):
        total = None
        for k in range(3):
            if c[k] == 0:
                continue
            term = v[k] if c[k] == 1 else -v[k]
            total = term if total is None else total + term
        return total

    base, dotted = common
    kept = (1.0 - 1.0 / relax_time) * pop
    scale = (1.0 - 0.5 / relax_time) * w
    if q == 0:
        return kept + (w / relax_time) * rho * base - (3.0 * scale) * dotted
    along = dot(u)
    pushed = dot(force)
    balance = (w / relax_time) * rho * (base + along * (3.0 + 4.5 * along))
    source = (3.0 * scale) * (pushed * (1.0 + 3.0 * along) - dotted)
    return kept + balance + source


def main_kernel(pops, mix, sides, react_in, pairs, spread, from_down, from_up, from_left, from_right, moved_out, out,
                moved, sems, ext, tside, tflat, tcorner, xtable, flo, fhi, post, gb, sacc, fe, *, cx, cy, nz, slots):
    chunks = slots // LANES
    wide = cx + 2
    mom, own, _, _ = views(mix, cx, cy, nz, chunks)

    ext[...] = jnp.zeros_like(ext)
    for c in range(3):
        for x in range(cx):
            ext[x + 2, c, 0:2, :] = from_down[2 * c : 2 * c + 2, x, :]
            ext[x + 2, c, 2 + cy : 4 + cy, :] = from_up[2 * c : 2 * c + 2, x, :]
        for x in (0, 1, cx - 2, cx - 1):
            ext[x + 2, c, 2 : 2 + cy, :] = mom[c, x]
        for x in range(2, cx - 2):
            ext[x + 2, c, 2 : 2 + SUB - 2, :] = mom[c, x, 0 : SUB - 2, :]
            ext[x + 2, c, 2 * SUB : 2 + cy, :] = mom[c, x, 2 * SUB - 2 : cy, :]
        for k in range(2):
            ext[k, c] = from_left[2 * c + k]
            ext[cx + 2 + k, c] = from_right[2 * c + k]
    for n, x in ((0, 0), (1, cx + 1)):
        tside[n] = both(ext[x : x + 3], 9 * YPAD, 9 * YPAD + SUB)
        for m, y in ((0, 0), (1, 2 * SUB)):
            tcorner[2 * n + m] = both(ext[x : x + 3, :, y : y + SUB, :], 9 * SUB, 10 * SUB)
    for m, y in ((0, 0), (1, 2 * SUB)):
        tflat[m] = both(ext[1 : cx + 3, :, y : y + SUB, :], wide * 3 * SUB)
    xtable[...] = both(jnp.concatenate([ext[1:2], ext[cx + 2 : cx + 3]], axis=0), 6 * YPAD)
    fe[...] = spread[...]
    flo[...] = jnp.zeros_like(flo)
    fhi[...] = jnp.zeros_like(fhi)

    def y_tile(ref):
        return lambda k: ref[STRIP + k]

    def x_tile(ref, part):
        def at(k):
            row = lax.rem(k, 3) * SUB
            return ref[STRIP + part * (chunks // 3 + 1) + lax.div(k, 3), pl.ds(pl.multiple_of(row, SUB), SUB), :]

        def first(k):
            if isinstance(k, int):
                return ref[STRIP + part * (chunks // 3 + 1) + k // 3, (k % 3) * SUB : (k % 3 + 1) * SUB, :]
            return at(k)

        return first

    sets = [(0, -1, y_tile(from_down)), (0, 1, y_tile(from_up))]
    for a, ref in ((-1, from_left), (1, from_right)):
        for part, b in enumerate((0, -1, 1)):
            sets.append((a, b, x_tile(ref, part)))
    counts = [jnp.max(source(0)[7:8, :]).astype(jnp.int32) for _, _, source in sets]
    own_count = jnp.max(own[0, 7:8, :]).astype(jnp.int32)
    own_chunks = chunks_of(own_count)

    def own_step(n, carry):
        for k in [n * UNROLL + u for u in range(UNROLL)]:
            tile = own[k]
            wx = tent(2 * SUB, -1.0, tile[0:1])
            wy = tent(YPAD, -2.0, tile[1:2])
            full = gather_rows(xtable[...], sample_table(*along_z(tile, nz))).reshape(2, 3, YPAD, LANES)
            total = full[0] * wx[0:1] + full[1] * wx[cx + 1 : cx + 2]
            sacc[k, 0:3, :] = friction * jnp.sum(total * wy[None], axis=1) - react_in[k, 0:3, :]
        return carry

    lax.fori_loop(0, steps_of(own_count), own_step, 0)

    jobs = []
    for (a, b, source), count in zip(sets, counts):
        side = 0 if a == -1 else 1
        half = 0 if b == -1 else 1
        if b == 0:
            depth, first_y, target = YPAD, -2.0, fe
        else:
            depth, first_y, target = SUB, -2.0 + 2 * SUB * half, (flo, fhi)[half]
        if a == 0:
            first_x, cols, slots_x = -1.0, wide, [(x, x) for x in range(wide)]
            table = tflat.at[half]
        else:
            cols = 3
            first_x = -2.0 if a == -1 else float(cx - 1)
            slots_x = [(0, 1), (1, 2)] if a == -1 else [(cx, 0), (cx + 1, 1)]
            table = tside.at[side] if b == 0 else tcorner.at[2 * side + half]
        jobs.append((source, count, float(a * cx), float(b * cy), table, cols, first_x, depth, first_y, slots_x,
                     target, False))
    for side, n in ((0, 1), (1, 0)):
        first_x = -2.0 if side == 0 else float(cx - 1)
        slots_x = [(0, 1), (1, 2)] if side == 0 else [(cx, 0), (cx + 1, 1)]
        source = lambda k, n=n: sides[n, k]
        count = jnp.max(sides[n, 0, 7:8, :]).astype(jnp.int32)
        jobs.append((source, count, 0.0, 0.0, xtable, 1, first_x, YPAD, -2.0, slots_x, fe, True))

    def reaction(job, k):
        source, _, shift_x, shift_y, table, cols, first_x, depth, first_y, _, _, own_list = job
        tile = source(k)
        high, low = along_z(tile, nz)
        wx = tent(2 * SUB, first_x, tile[0:1] + shift_x)
        wy = tent(depth, first_y, tile[1:2] + shift_y)
        right = sample_table(high, low)
        if own_list:
            at = 0 if first_x < 0.0 else 3 * YPAD
            row = 1
            full = gather_rows(xtable[...], right)[at : at + 3 * YPAD].reshape(1, 3, YPAD, LANES)
            total = full[0] * wx[row : row + 1]
            react = -friction * jnp.sum(total * wy[None], axis=1)
        else:
            full = gather_rows(table[...], right)[: cols * 3 * depth].reshape(cols, 3, depth, LANES)
            total = full[0] * wx[0:1]
            for x in range(1, cols):
                total = total + full[x] * wx[x : x + 1]
            react = tile[3:6] - friction * jnp.sum(total * wy[None], axis=1)
        return react * tile[6:7], wx, wy, high, low

    def spread_job(job, parts):
        react, wx, wy, high, low = parts
        depth, slots_x = job[7], job[9]
        pieces = []
        for _, w in slots_x:
            for c in range(3):
                pieces.append((wx[w : w + 1] * react[c : c + 1]) * wy)
        got = spread_rows(both(jnp.stack(pieces), len(slots_x) * 3 * depth), high, low)
        return got.reshape(len(slots_x), 3, depth, LANES)

    def add_job(job, got):
        for n, (f, _) in enumerate(job[9]):
            job[10][f] += got[n]

    parts = [reaction(job, 0) for job in jobs]
    gots = [spread_job(job, part) for job, part in zip(jobs, parts)]
    for job, got in zip(jobs, gots):
        add_job(job, got)
    for job in jobs:

        def more(k, carry, job=job):
            add_job(job, spread_job(job, reaction(job, k)))
            return carry

        lax.fori_loop(1, chunks_of(job[1]), more, 0)

    for x in range(wide):
        fe[x, :, 0:SUB, :] += flo[x]
        fe[x, :, 2 * SUB : 3 * SUB, :] += fhi[x]

    base_row = SUB

    def prepared(rho, u0, force):
        half = 0.5 / rho
        u = [u0[c] + half * force[c] for c in range(3)]
        base = 1.0 - 1.5 * (u[0] * u[0] + u[1] * u[1] + u[2] * u[2])
        dotted = u[0] * force[0] + u[1] * force[1] + u[2] * force[2]
        return u, (base, dotted)

    for x in range(cx):
        for h in range(0, cy, SUB):
            force = [fe[x + 1, c, 2 + h : 2 + h + SUB, :] for c in range(3)]
            rho = mom[3, x, h : h + SUB, :]
            u, common = prepared(rho, [mom[c, x, h : h + SUB, :] for c in range(3)], force)
            for q in range(19):
                post[q, x + 1, base_row + h : base_row + h + SUB, :] = post_of(
                    q, pops[q, x, h : h + SUB, :], rho, u, force, common
                )
    for ref, row, layer, sign in ((from_left, 0, 1, 1), (from_right, cx + 1, 0, -1)):
        force = [fe[row, c] for c in range(3)]
        rho = ref[6]
        u, common = prepared(rho, [ref[2 * c + layer] for c in range(3)], force)
        for k, q in enumerate(outward(0, sign)):
            post[q, row, base_row - 2 : base_row - 2 + YPAD, :] = post_of(q, ref[7 + k], rho, u, force, common)
    for ref, row, at, layer, sign in (
        (from_down, base_row - 1, 1, 1, 1),
        (from_up, base_row + cy, cy + 2, 0, -1),
    ):
        force = [fe[1 : 1 + cx, c, at, :] for c in range(3)]
        rho = ref[6]
        u, common = prepared(rho, [ref[2 * c + layer] for c in range(3)], force)
        for k, q in enumerate(outward(1, sign)):
            post[q, 1 : 1 + cx, row, :] = post_of(q, ref[7 + k], rho, u, force, common)
    copies = []
    for q in range(19):
        dx, dy, dz = lattice_dirs[q]
        for x in range(cx):
            plane = post[q, x + 1 - dx, base_row - dy : base_row - dy + cy, :]
            if dz != 0:
                plane = pltpu.roll(plane, dz % nz, 1)
            moved[q, x] = plane
        copies.append(pltpu.make_async_copy(moved.at[q], moved_out.at[q], sems.at[q]))
        copies[-1].start()

    at = jnp.int32(0)
    for (a, b, source), count in zip(sets, counts):
        ghost_rows(gb, source(0), at, float(a * cx), float(b * cy), nz)

        def fill(k, carry, source=source, a=a, b=b, at=at):
            ghost_rows(gb, source(k), at + k * LANES, float(a * cx), float(b * cy), nz)
            return carry

        lax.fori_loop(1, chunks_of(count), fill, 0)
        at = at + lax.div(count + (SUB - 1), SUB) * SUB
    gb[0, pl.ds(pl.multiple_of(at, SUB), GROUP * SUB), :] = jnp.full((GROUP * SUB, LANES), FAR, f32)
    groups = lax.div(at + (GROUP * SUB - 1), GROUP * SUB)

    def pair_step(k, carry):
        total = pair_rows(gb, own[k], groups, tuple(pairs[k, c] for c in range(3)), nz)
        sums = jnp.concatenate([jnp.sum(t, axis=0, keepdims=True) for t in total], axis=0)
        sacc[k, 0:3, :] = sacc[k, 0:3, :] + (48.0 * wca_energy) * sums
        return carry

    lax.fori_loop(0, own_chunks, pair_step, 0)

    for c in range(3):
        out[c * chunks : (c + 1) * chunks, :] = jnp.where(own[:, 6, :] > 0.0, sacc[:, c, :], 0.0)
    for copy in copies:
        copy.wait()


def shifted(value, axis, by):
    devices = lax.axis_size(axis)
    return lax.ppermute(value, axis, [(i, (i + by) % devices) for i in range(devices)])


def body(populations, anchor, offsets, heading, velocity, live_count):
    _, cx, cy, nz = populations.shape
    slots = anchor.shape[2]
    chunks = slots // LANES
    sizes = dict(cx=cx, cy=cy, nz=nz, slots=slots)
    vmem = pl.BlockSpec(memory_space=pltpu.VMEM)
    smem = pl.BlockSpec(memory_space=pltpu.SMEM)
    shape = jax.ShapeDtypeStruct

    hbm = pl.BlockSpec(memory_space=pltpu.HBM)

    def call(kernel, name, outs, scratch, *args, ins=None, out_specs=None, limit=48):
        return pl.pallas_call(
            functools.partial(kernel, **sizes),
            out_shape=outs,
            in_specs=ins or [vmem] * len(args),
            out_specs=out_specs or (vmem,) * len(outs),
            scratch_shapes=scratch,
            compiler_params=pltpu.CompilerParams(vmem_limit_bytes=limit * 2**20),
            name=name,
        )(*args)

    face_y = shape((STRIP + chunks, cx, nz), f32)
    tiles = shape((chunks, SUB, LANES), f32)
    dma = pltpu.SemaphoreType.DMA
    mix, up, down = call(
        pack_y, "pack_y",
        (shape((4 * cx * cy + (SUB + 4) * chunks + 10 * cy, LANES), f32), face_y, face_y),
        [
            pltpu.VMEM(populations.shape, f32),
            pltpu.VMEM((chunks, LANES), jnp.int32),
            pltpu.VMEM((3 * chunks, LANES), f32),
            pltpu.VMEM((2, slots), f32),
            pltpu.VMEM((3 * chunks, LANES), f32),
            pltpu.VMEM((2, chunks, LANES), f32),
            dma((5,)),
        ],
        populations, anchor.reshape(chunks, LANES), offsets.reshape(3 * chunks, LANES), heading[0, 0],
        velocity.reshape(3 * chunks, LANES), live_count, ins=[hbm] * 5 + [smem], limit=62,
    )
    from_down = shifted(up, "gy", 1)
    from_up = shifted(down, "gy", -1)
    part, sides = call(
        own_first, "own_first",
        (tiles, shape((2, chunks, SUB, LANES), f32)),
        [pltpu.VMEM((3 * cx * cy, 2 * nz), bf16)],
        mix,
    )
    face_x = shape((STRIP + 3 * (chunks // 3 + 1), YPAD, nz), f32)
    right, left = call(
        pack_x, "pack_x", (face_x, face_x), [], mix, sides, from_down, from_up,
    )
    from_left = shifted(right, "gx", 1)
    from_right = shifted(left, "gx", -1)
    wide = cx + 2
    spread, react, pairs = call(
        own_second, "own_second",
        (shape((wide, 3, YPAD, nz), f32), tiles, shape((chunks, 3, SUB, LANES), f32)),
        [pltpu.VMEM((3, slots, LANES), f32), pltpu.VMEM((6 * cx, 2 * nz), bf16)],
        mix, part, from_down, from_up,
    )
    moved, force = call(
        main_kernel, "main",
        (shape(populations.shape, f32), shape((3 * chunks, LANES), f32)),
        [
            pltpu.VMEM(populations.shape, f32),
            dma((19,)),
            pltpu.VMEM((cx + 4, 3, YPAD, nz), f32),
            pltpu.VMEM((2, 9 * YPAD + SUB, 2 * nz), bf16),
            pltpu.VMEM((2, wide * 3 * SUB, 2 * nz), bf16),
            pltpu.VMEM((4, 10 * SUB, 2 * nz), bf16),
            pltpu.VMEM((6 * YPAD, 2 * nz), bf16),
            pltpu.VMEM((wide, 3, SUB, nz), f32),
            pltpu.VMEM((wide, 3, SUB, nz), f32),
            pltpu.VMEM((19, cx + 2, cy + 2 * SUB, nz), f32),
            pltpu.VMEM((3, 8 * slots + LANES, LANES), f32),
            pltpu.VMEM((chunks, SUB, LANES), f32),
            pltpu.VMEM((wide, 3, YPAD, nz), f32),
        ],
        populations, mix, sides, react, pairs, spread, from_down, from_up, from_left, from_right,
        out_specs=(hbm, vmem),
    )
    return moved, force.reshape(1, 1, 3, slots)


def solution(mesh):
    return jax.shard_map(
        body,
        mesh=mesh,
        in_specs=(
            P(None, "gx", "gy", None),
            P("gx", "gy", None),
            P("gx", "gy", None, None),
            P("gx", "gy", None, None),
            P("gx", "gy", None, None),
            P("gx", "gy"),
        ),
        out_specs=(P(None, "gx", "gy", None), P("gx", "gy", None, None)),
        check_vma=False,
    )
```

profile of v0, /device:TPU:9, one launch (start us, length us, event | category | flops | bytes accessed | tf_op | source)
XLA Modules:
  0.0 30.2 jit_solution(9736312656741233648)
XLA Ops:
  1.3 0.0 copy-start.2
  1.3 3.0 %pack_y.1 = (f32[768,128]{1,0:T(8,128)}, f32[20,8,128]{2,1,0:T(8,128)}, f32[20,8,128]{2,1,0:T(8,128)}) custom-call(f32[19,8,16,128]{3,2,1,0:T(8,128)} %pops.1, s32[8,128]{1,0:T(8,128)} %bitcast.8, f32[24,128]{1,0:T(8,128)} %bitcast.5, f32[2,1024]{1,0:T(2,128)} %bitcast.7, f32[24,128]{1,0:T(8,128)} %bitcast.6, s32[1,1]{1,0:T(1,128)S(6)} %copy.10.count), custom_call_target="tpu_custom_call" | custom-call | tf_op jit(solution)/shard_map/pack_y/pallas_call | solution.py:671
  4.3 0.9 %collective-permute-start = (f32[20,8,128]{2,1,0:T(8,128)}, f32[20,8,128]{2,1,0:T(8,128)S(1)}, u32[]{:S(2)}, u32[]{:S(2)}) collective-permute-start(f32[20,8,128]{2,1,0:T(8,128)} %get-tuple-element.17), channel_id=1, source_target_pairs={{0,1},{1,2},{2,3},{3,0},{4,5},{5,6},{6,7},{7,4},{8,9},{9,10},{10,1... | collective-permute-start | bytes 245768 | tf_op jit(solution)/shard_map/ppermute | solution.py:656
  5.2 0.6 %collective-permute-start.1 = (f32[20,8,128]{2,1,0:T(8,128)}, f32[20,8,128]{2,1,0:T(8,128)S(1)}, u32[]{:S(2)}, u32[]{:S(2)}) collective-permute-start(f32[20,8,128]{2,1,0:T(8,128)} %get-tuple-element.18), channel_id=1, source_target_pairs={{0,3},{1,0},{2,1},{3,2},{4,7},{5,4},{6,5},{7,6},{8,11},{9,8},{10,9... | collective-permute-start | bytes 245768 | tf_op jit(solution)/shard_map/ppermute | solution.py:656
  5.8 0.0 copy-start
  5.8 1.0 %copy-done = f32[768,128]{1,0:T(8,128)S(1)} copy-done((f32[768,128]{1,0:T(8,128)S(1)}, f32[768,128]{1,0:T(8,128)}, u32[]{:S(2)}) %copy-start) | copy-done | bytes 393240
  6.8 0.0 copy-start.1
  6.8 2.2 %own_first.1 = (f32[8,8,128]{2,1,0:T(8,128)S(1)}, f32[2,8,8,128]{3,2,1,0:T(8,128)S(1)}) custom-call(f32[768,128]{1,0:T(8,128)S(1)} %copy-done), custom_call_target="tpu_custom_call" | custom-call | tf_op jit(solution)/shard_map/own_first/pallas_call | solution.py:671
  8.9 0.0 collective-permute-done.from_down
  9.0 2.0 %collective-permute-done.1.from_up = f32[20,8,128]{2,1,0:T(8,128)S(1)} collective-permute-done((f32[20,8,128]{2,1,0:T(8,128)}, f32[20,8,128]{2,1,0:T(8,128)S(1)}, u32[]{:S(2)}, u32[]{:S(2)}) %collective-permute-start.1) | collective-permute-done | bytes 81952 | tf_op jit(solution)/shard_map/ppermute | solution.py:656
  11.0 0.1 pack_x.1
  11.0 1.8 %collective-permute-start.2 = (f32[21,24,128]{2,1,0:T(8,128)S(1)}, f32[21,24,128]{2,1,0:T(8,128)S(1)}, u32[]{:S(2)}, u32[]{:S(2)}) collective-permute-start(f32[21,24,128]{2,1,0:T(8,128)S(1)} %get-tuple-element.22), channel_id=1, source_target_pairs={{0,4},{4,8},{8,12},{12,16},{16,20},{20,24},{24,28},{28,0},{1,5},{5... | collective-permute-start | bytes 774152 | tf_op jit(solution)/shard_map/ppermute | solution.py:656
  12.8 0.0 collective-permute-start.3
  12.8 8.7 %own_second.1 = (f32[10,3,24,128]{3,2,1,0:T(8,128)S(1)}, f32[8,8,128]{2,1,0:T(8,128)S(1)}, f32[8,3,8,128]{3,2,1,0:T(8,128)S(1)}) custom-call(f32[768,128]{1,0:T(8,128)S(1)} %copy-done, f32[8,8,128]{2,1,0:T(8,128)S(1)} %get-tuple-element.16.part, f32[20,8,128]{2,1,0:T(8,128)S(1)} %collective-permute-done.from_down, ...), custom_call_target="tpu_custom_call" | custom-call | tf_op jit(solution)/shard_map/own_second/pallas_call | solution.py:671
  21.5 0.0 collective-permute-done.2.from_left
  21.5 0.0 collective-permute-done.3.from_right
  21.5 0.0 copy-done.2
  21.6 0.0 copy-done.1
  21.6 8.7 %main.1 = (f32[19,8,16,128]{3,2,1,0:T(8,128)}, f32[24,128]{1,0:T(8,128)}) custom-call(f32[19,8,16,128]{3,2,1,0:T(8,128)S(1)} %copy-done.2, f32[768,128]{1,0:T(8,128)S(1)} %copy-done.1, f32[2,8,8,128]{3,2,1,0:T(8,128)S(1)} %get-tuple-element.15.sides, f32[8,8,128]{2,1,0:T(8,128)S(1)} %get-tuple-element.19.react_in, ...), custom_call_target="tpu_custom_call" | custom-call | tf_op jit(solution)/shard_map/main/pallas_call | solution.py:671
Async XLA Ops:
  1.3 20.3 %copy-start.2 = (f32[19,8,16,128]{3,2,1,0:T(8,128)S(1)}, f32[19,8,16,128]{3,2,1,0:T(8,128)}, u32[]{:S(2)}) copy-start(f32[19,8,16,128]{3,2,1,0:T(8,128)} %pops.1) | copy-start | bytes 3735556
  4.3 4.7 %collective-permute-start = (f32[20,8,128]{2,1,0:T(8,128)}, f32[20,8,128]{2,1,0:T(8,128)S(1)}, u32[]{:S(2)}, u32[]{:S(2)}) collective-permute-start(f32[20,8,128]{2,1,0:T(8,128)} %get-tuple-element.17), channel_id=1, source_target_pairs={{0,1},{1,2},{2,3},{3,0},{4,5},{5,6},{6,7},{7,4},{8,9},{9,10},{10,1... | collective-permute-start | bytes 245768 | tf_op jit(solution)/shard_map/ppermute | solution.py:656
  5.2 5.8 %collective-permute-start.1 = (f32[20,8,128]{2,1,0:T(8,128)}, f32[20,8,128]{2,1,0:T(8,128)S(1)}, u32[]{:S(2)}, u32[]{:S(2)}) collective-permute-start(f32[20,8,128]{2,1,0:T(8,128)} %get-tuple-element.18), channel_id=1, source_target_pairs={{0,3},{1,0},{2,1},{3,2},{4,7},{5,4},{6,5},{7,6},{8,11},{9,8},{10,9... | collective-permute-start | bytes 245768 | tf_op jit(solution)/shard_map/ppermute | solution.py:656
  5.8 1.0 %copy-start = (f32[768,128]{1,0:T(8,128)S(1)}, f32[768,128]{1,0:T(8,128)}, u32[]{:S(2)}) copy-start(f32[768,128]{1,0:T(8,128)} %get-tuple-element.14.mix) | copy-start | bytes 1179652
  6.8 14.8 %copy-start.1 = (f32[768,128]{1,0:T(8,128)S(1)}, f32[768,128]{1,0:T(8,128)}, u32[]{:S(2)}) copy-start(f32[768,128]{1,0:T(8,128)} %get-tuple-element.14.mix) | copy-start | bytes 1179652
  11.0 10.5 %collective-permute-start.2 = (f32[21,24,128]{2,1,0:T(8,128)S(1)}, f32[21,24,128]{2,1,0:T(8,128)S(1)}, u32[]{:S(2)}, u32[]{:S(2)}) collective-permute-start(f32[21,24,128]{2,1,0:T(8,128)S(1)} %get-tuple-element.22), channel_id=1, source_target_pairs={{0,4},{4,8},{8,12},{12,16},{16,20},{20,24},{24,28},{28,0},{1,5},{5... | collective-permute-start | bytes 774152 | tf_op jit(solution)/shard_map/ppermute | solution.py:656
  12.8 8.8 %collective-permute-start.3 = (f32[21,24,128]{2,1,0:T(8,128)S(1)}, f32[21,24,128]{2,1,0:T(8,128)S(1)}, u32[]{:S(2)}, u32[]{:S(2)}) collective-permute-start(f32[21,24,128]{2,1,0:T(8,128)S(1)} %get-tuple-element.23), channel_id=1, source_target_pairs={{0,28},{4,0},{8,4},{12,8},{16,12},{20,16},{24,20},{28,24},{1,29},{... | collective-permute-start | bytes 774152 | tf_op jit(solution)/shard_map/ppermute | solution.py:656
where the time goes:
time: 30.5 us; the launch traced here: 30.2 us
  Pallas kernels  22.6 us (74%)
  starting transfers between devices  3.29 us (11%)
  waiting for transfers between devices  2 us (7%)
  between operations  1.35 us (4%)
  local copies, waits for them, and re-layouts  1 us (3%)
    pallas_call x5, Pallas kernels, call(): pl.pallas_call(functools.partial(kernel, **sizes), out_shape=outs, in_spe...  22.6 us
    ppermute x4, starting transfers between devices, shifted(): lax.ppermute(value, axis, [(i, (i + by) % devices) for i in range(devices)])  3.29 us
    ppermute x4, waiting for transfers between devices, shifted(): lax.ppermute(value, axis, [(i, (i + by) % devices) for i in range(devices)])  2 us
    unnamed x6, local copies, waits for them, and re-layouts  1 us
  transfers between devices with their start and end apart: 4, of which 1 were waited for; matrix products, arithmetic and copies ran while one was open for 0% of the time, Pallas kernels for 36%

commit v1 on v0

--- a/solution.py
+++ b/solution.py
@@ -102,7 +102,7 @@
     return lax.div(count + (LANES - 1), LANES)
 
 
-UNROLL = 2
+UNROLL = 4
 
 
 def steps_of(count):
@@ -181,11 +181,18 @@
     masks = [
         jnp.where(place_y > cy - 1 - REACH, alive, 0.0),
         jnp.where(place_y < REACH, alive, 0.0),
-        jnp.where(place_x > cx - 1 - REACH, alive, 0.0),
-        jnp.where(place_x < REACH, alive, 0.0),
+        jnp.where(place_x >= cx - 1, alive, 0.0),
+        jnp.where((place_x > cx - 1 - REACH) & (place_x < cx - 1), alive, 0.0),
+        jnp.where(place_x < 0.0, alive, 0.0),
+        jnp.where((place_x < REACH) & (place_x >= 0.0), alive, 0.0),
     ]
     place = ranks_of(jnp.concatenate(masks, axis=0), chunks)
-    ranks[...] = place
+    ranks[0 : 2 * chunks, :] = place[0 : 2 * chunks]
+    for n in (2, 3):
+        ahead = place[(2 * n - 2) * chunks : (2 * n - 1) * chunks]
+        after = place[(2 * n - 1) * chunks : 2 * n * chunks]
+        begin = jnp.max(jnp.max(ahead, axis=1, keepdims=True), axis=0, keepdims=True) + 1.0
+        ranks[n * chunks : (n + 1) * chunks, :] = jnp.where(after >= 0.0, after + begin, ahead)
     parts = thirds(jnp.concatenate([own[k] for k in range(chunks)], axis=1))
     for n, ref in ((0, up), (1, down)):
         rank = place[n * chunks : (n + 1) * chunks]
@@ -252,7 +259,62 @@
     return spread_many([left], [high, high], [low, low])
 
 
-def own_first(mix, part, sides, table, *, cx, cy, nz, slots):
+def turns(z, nz):
+    return ((z - 0.5 * nz) * (2.0**32 / nz)).astype(jnp.int32)
+
+
+def ghost_rows(gb, gz, tile, at, shift_x, shift_y, nz):
+    flat = jnp.transpose(tile)
+    rows = pl.ds(pl.multiple_of(at, SUB), LANES)
+    gb[0, rows, :] = jnp.broadcast_to(flat[:, 0:1] + shift_x, (LANES, LANES))
+    gb[1, rows, :] = jnp.broadcast_to(flat[:, 1:2] + shift_y, (LANES, LANES))
+    gz[rows, :] = turns(jnp.broadcast_to(flat[:, 2:3], (LANES, LANES)), nz)
+
+
+GROUP = 16
+
+
+def pair_rows(gb, gz, tile, rows, total, nz):
+    px, py = (jnp.broadcast_to(tile[c : c + 1], (SUB, LANES)) for c in range(2))
+    pz = turns(jnp.broadcast_to(tile[2:3], (SUB, LANES)), nz)
+
+    def step(g, total):
+        fx, fy, fz = total
+        for r in range(GROUP):
+            at = pl.ds(pl.multiple_of((g * GROUP + r) * SUB, SUB), SUB)
+            dx = px - gb[0, at, :]
+            dy = py - gb[1, at, :]
+            dz = (pz - gz[at, :]).astype(f32) * (nz / 2.0**32)
+            raw = dx * dx + dy * dy + dz * dz
+            square = jnp.maximum(raw, floor_square)
+            inverse = pl.reciprocal(square, approx=True)
+            sixth = inverse * inverse * inverse
+            size = (sixth * inverse) * jnp.maximum(sixth - 0.5, 0.0)
+            fx = fx + size * dx
+            fy = fy + size * dy
+            fz = fz + size * dz
+        return fx, fy, fz
+
+    return lax.fori_loop(0, rows, step, total)
+
+
+EARLY = 2
+
+
+def own_pairs(own, gb, gz, pairs, first, last, count, nz):
+    groups = lax.div(count + (GROUP * SUB - 1), GROUP * SUB)
+
+    def own_step(k, carry):
+        zero = jnp.zeros((SUB, LANES), f32)
+        total = pair_rows(gb, gz, own[k], groups, (zero, zero, zero), nz)
+        for c in range(3):
+            pairs[k, c] = total[c]
+        return carry
+
+    lax.fori_loop(first, last, own_step, 0)
+
+
+def own_first(mix, part, sides, gb, gz, early, table, *, cx, cy, nz, slots):
     chunks = slots // LANES
     mom, own, ranks, _ = views(mix, cx, cy, nz, chunks)
     fields = jnp.concatenate([own[k] for k in range(chunks)], axis=1)
@@ -286,6 +348,14 @@
 
     count = jnp.max(own[0, 7:8, :]).astype(jnp.int32)
     lax.fori_loop(0, steps_of(count), step, 0)
+
+    def fill(n, carry):
+        for k in [n * UNROLL + u for u in range(UNROLL)]:
+            ghost_rows(gb, gz, own[k], k * LANES, 0.0, 0.0, nz)
+        return carry
+
+    lax.fori_loop(0, steps_of(count), fill, 0)
+    own_pairs(own, gb, gz, early, 0, jnp.minimum(chunks_of(count), EARLY), count, nz)
 
 
 def pack_x(mix, sides, from_down, from_up, right, left, *, cx, cy, nz, slots):
@@ -319,45 +389,7 @@
                 ref[STRIP + part * (chunks // 3 + 1) + k // 3, (k % 3) * SUB : (k % 3 + 1) * SUB, :] = tile
 
 
-def ghost_rows(gb, tile, at, shift_x, shift_y, nz):
-    flat = jnp.transpose(tile)
-    rows = pl.ds(pl.multiple_of(at, SUB), LANES)
-    gb[0, rows, :] = jnp.broadcast_to(flat[:, 0:1] + shift_x, (LANES, LANES))
-    gb[1, rows, :] = jnp.broadcast_to(flat[:, 1:2] + shift_y, (LANES, LANES))
-    gb[2, rows, :] = jnp.broadcast_to(flat[:, 2:3] * (1.0 / nz), (LANES, LANES))
-
-
-GROUP = 16
-
-
-def pair_rows(gb, tile, rows, total, nz):
-    px, py = (jnp.broadcast_to(tile[c : c + 1], (SUB, LANES)) for c in range(2))
-    pz = jnp.broadcast_to(tile[2:3] * (1.0 / nz), (SUB, LANES))
-
-    def step(g, total):
-        fx, fy, fz = total
-        for r in range(GROUP):
-            at = pl.ds(pl.multiple_of((g * GROUP + r) * SUB, SUB), SUB)
-            dx = px - gb[0, at, :]
-            dy = py - gb[1, at, :]
-            dz = pz - gb[2, at, :]
-            dz = (dz - jnp.round(dz)) * float(nz)
-            raw = dx * dx + dy * dy + dz * dz
-            square = jnp.maximum(raw, floor_square)
-            inverse = pl.reciprocal(square, approx=True)
-            inverse = inverse * (2.0 - square * inverse)
-            sixth = inverse * inverse * inverse
-            size = (sixth * (sixth - 0.5)) * inverse
-            size = jnp.where(raw < cutoff_square, size, 0.0)
-            fx = fx + size * dx
-            fy = fy + size * dy
-            fz = fz + size * dz
-        return fx, fy, fz
-
-    return lax.fori_loop(0, rows, step, total)
-
-
-def own_second(mix, part, from_down, from_up, spread_out, react_out, pairs, gb, ytable, *, cx, cy, nz, slots):
+def own_second(mix, part, gb, gz, early, from_down, from_up, spread_out, react_out, pairs, ytable, *, cx, cy, nz, slots):
     chunks = slots // LANES
     _, own, _, _ = views(mix, cx, cy, nz, chunks)
     count = jnp.max(own[0, 7:8, :]).astype(jnp.int32)
@@ -395,23 +427,8 @@
 
     lax.fori_loop(0, steps_of(count), step, 0)
 
-    pairs[...] = jnp.zeros_like(pairs)
-
-    def fill(k, carry):
-        ghost_rows(gb, own[k], k * LANES, 0.0, 0.0, nz)
-        return carry
-
-    lax.fori_loop(0, live_chunks, fill, 0)
-    groups = lax.div(count + (GROUP * SUB - 1), GROUP * SUB)
-
-    def own_step(k, carry):
-        zero = jnp.zeros((SUB, LANES), f32)
-        total = pair_rows(gb, own[k], groups, (zero, zero, zero), nz)
-        for c in range(3):
-            pairs[k, c] = total[c]
-        return carry
-
-    lax.fori_loop(0, live_chunks, own_step, 0)
+    pairs[0:EARLY] = early[...]
+    own_pairs(own, gb, gz, pairs, EARLY, live_chunks, count, nz)
 
 
 def post_of(q, pop, rho, u, force, common):
@@ -440,7 +457,7 @@
 
 
 def main_kernel(pops, mix, sides, react_in, pairs, spread, from_down, from_up, from_left, from_right, moved_out, out,
-                moved, sems, ext, tside, tflat, tcorner, xtable, flo, fhi, post, gb, sacc, fe, *, cx, cy, nz, slots):
+                moved, sems, ext, tside, tflat, tcorner, xtable, flo, fhi, post, gb, gz, sacc, fe, *, cx, cy, nz, slots):
     chunks = slots // LANES
     wide = cx + 2
     mom, own, _, _ = views(mix, cx, cy, nz, chunks)
@@ -526,7 +543,8 @@
         first_x = -2.0 if side == 0 else float(cx - 1)
         slots_x = [(0, 1), (1, 2)] if side == 0 else [(cx, 0), (cx + 1, 1)]
         source = lambda k, n=n: sides[n, k]
-        count = jnp.max(sides[n, 0, 7:8, :]).astype(jnp.int32)
+        near = (own[:, 0, :] < 0.0) if side == 0 else (own[:, 0, :] >= cx - 1)
+        count = jnp.sum(jnp.where(near, own[:, 6, :], 0.0)).astype(jnp.int32)
         jobs.append((source, count, 0.0, 0.0, xtable, 1, first_x, YPAD, -2.0, slots_x, fe, True))
 
     def reaction(job, k):
@@ -625,20 +643,23 @@
         copies[-1].start()
 
     at = jnp.int32(0)
+    places = []
     for (a, b, source), count in zip(sets, counts):
-        ghost_rows(gb, source(0), at, float(a * cx), float(b * cy), nz)
-
-        def fill(k, carry, source=source, a=a, b=b, at=at):
-            ghost_rows(gb, source(k), at + k * LANES, float(a * cx), float(b * cy), nz)
+        ghost_rows(gb, gz, source(0), at, float(a * cx), float(b * cy), nz)
+        places.append(at)
+        at = at + jnp.where(count > LANES, chunks_of(count) * LANES, lax.div(count + (SUB - 1), SUB) * SUB)
+    for (a, b, source), count, begin in zip(sets, counts, places):
+
+        def fill(k, carry, source=source, a=a, b=b, begin=begin):
+            ghost_rows(gb, gz, source(k), begin + k * LANES, float(a * cx), float(b * cy), nz)
             return carry
 
         lax.fori_loop(1, chunks_of(count), fill, 0)
-        at = at + lax.div(count + (SUB - 1), SUB) * SUB
     gb[0, pl.ds(pl.multiple_of(at, SUB), GROUP * SUB), :] = jnp.full((GROUP * SUB, LANES), FAR, f32)
     groups = lax.div(at + (GROUP * SUB - 1), GROUP * SUB)
 
     def pair_step(k, carry):
-        total = pair_rows(gb, own[k], groups, tuple(pairs[k, c] for c in range(3)), nz)
+        total = pair_rows(gb, gz, own[k], groups, tuple(pairs[k, c] for c in range(3)), nz)
         sums = jnp.concatenate([jnp.sum(t, axis=0, keepdims=True) for t in total], axis=0)
         sacc[k, 0:3, :] = sacc[k, 0:3, :] + (48.0 * wca_energy) * sums
         return carry
@@ -698,9 +719,10 @@
     )
     from_down = shifted(up, "gy", 1)
     from_up = shifted(down, "gy", -1)
-    part, sides = call(
+    part, sides, gb, gz, early = call(
         own_first, "own_first",
-        (tiles, shape((2, chunks, SUB, LANES), f32)),
+        (tiles, shape((2, chunks, SUB, LANES), f32), shape((2, slots, LANES), f32), shape((slots, LANES), jnp.int32),
+         shape((EARLY, 3, SUB, LANES), f32)),
         [pltpu.VMEM((3 * cx * cy, 2 * nz), bf16)],
         mix,
     )
@@ -714,8 +736,8 @@
     spread, react, pairs = call(
         own_second, "own_second",
         (shape((wide, 3, YPAD, nz), f32), tiles, shape((chunks, 3, SUB, LANES), f32)),
-        [pltpu.VMEM((3, slots, LANES), f32), pltpu.VMEM((6 * cx, 2 * nz), bf16)],
-        mix, part, from_down, from_up,
+        [pltpu.VMEM((6 * cx, 2 * nz), bf16)],
+        mix, part, gb, gz, early, from_down, from_up,
     )
     moved, force = call(
         main_kernel, "main",
@@ -731,7 +753,8 @@
             pltpu.VMEM((wide, 3, SUB, nz), f32),
             pltpu.VMEM((wide, 3, SUB, nz), f32),
             pltpu.VMEM((19, cx + 2, cy + 2 * SUB, nz), f32),
-            pltpu.VMEM((3, 8 * slots + LANES, LANES), f32),
+            pltpu.VMEM((2, 8 * slots + LANES, LANES), f32),
+            pltpu.VMEM((8 * slots + LANES, LANES), jnp.int32),
             pltpu.VMEM((chunks, SUB, LANES), f32),
             pltpu.VMEM((wide, 3, YPAD, nz), f32),
         ],

time: 30.5 us -> 26.2 us (0.86)
  the two profiles are of different devices: /device:TPU:9 before, /device:TPU:1 now
where the time goes in v1:
time: 26.2 us; the launch traced here: 26 us
  Pallas kernels  9.37 us (36%)
  waiting for transfers between devices  7.72 us (29%)
  starting transfers between devices  6.53 us (25%)
  between operations  1.33 us (5%)
  local copies, waits for them, and re-layouts  1.01 us (4%)
    pallas_call x5, Pallas kernels, call(): pl.pallas_call(functools.partial(kernel, **sizes), out_shape=outs, in_spe...  9.37 us
    ppermute x4, waiting for transfers between devices, shifted(): lax.ppermute(value, axis, [(i, (i + by) % devices) for i in range(devices)])  7.72 us
    ppermute x4, starting transfers between devices, shifted(): lax.ppermute(value, axis, [(i, (i + by) % devices) for i in range(devices)])  6.53 us
    unnamed x6, local copies, waits for them, and re-layouts  1.01 us
  transfers between devices with their start and end apart: 4, of which 3 were waited for; matrix products, arithmetic and copies ran while one was open for 0% of the time, Pallas kernels for 10%

profile of v1, /device:TPU:1, one launch (start us, length us, event | category | flops | bytes accessed | tf_op | source)
XLA Modules:
  0.0 26.0 jit_solution(15611678141992484571)
XLA Ops:
  1.3 2.5 %pack_y.1 = (f32[768,128]{1,0:T(8,128)}, f32[20,8,128]{2,1,0:T(8,128)}, f32[20,8,128]{2,1,0:T(8,128)}) custom-call(f32[19,8,16,128]{3,2,1,0:T(8,128)} %pops.1, s32[8,128]{1,0:T(8,128)} %bitcast.8, f32[24,128]{1,0:T(8,128)} %bitcast.5, f32[2,1024]{1,0:T(2,128)} %bitcast.7, f32[24,128]{1,0:T(8,128)} %bitcast.6, s32[1,1]{1,0:T(1,128)S(6)} %copy.10.count), custom_call_target="tpu_custom_call" | custom-call | tf_op jit(solution)/shard_map/pack_y/pallas_call | solution.py:692
  3.8 2.2 %collective-permute-start = (f32[20,8,128]{2,1,0:T(8,128)}, f32[20,8,128]{2,1,0:T(8,128)S(1)}, u32[]{:S(2)}, u32[]{:S(2)}) collective-permute-start(f32[20,8,128]{2,1,0:T(8,128)} %get-tuple-element.23), channel_id=1, source_target_pairs={{0,1},{1,2},{2,3},{3,0},{4,5},{5,6},{6,7},{7,4},{8,9},{9,10},{10,1... | collective-permute-start | bytes 245768 | tf_op jit(solution)/shard_map/ppermute | solution.py:677
  5.9 2.1 %collective-permute-start.1 = (f32[20,8,128]{2,1,0:T(8,128)}, f32[20,8,128]{2,1,0:T(8,128)S(1)}, u32[]{:S(2)}, u32[]{:S(2)}) collective-permute-start(f32[20,8,128]{2,1,0:T(8,128)} %get-tuple-element.24), channel_id=1, source_target_pairs={{0,3},{1,0},{2,1},{3,2},{4,7},{5,4},{6,5},{7,6},{8,11},{9,8},{10,9... | collective-permute-start | bytes 245768 | tf_op jit(solution)/shard_map/ppermute | solution.py:677
  8.0 0.0 copy-start
  8.0 1.0 %copy-done = f32[768,128]{1,0:T(8,128)S(1)} copy-done((f32[768,128]{1,0:T(8,128)S(1)}, f32[768,128]{1,0:T(8,128)}, u32[]{:S(2)}) %copy-start) | copy-done | bytes 393240
  9.0 1.7 %own_first.1 = (f32[8,8,128]{2,1,0:T(8,128)S(1)}, f32[2,8,8,128]{3,2,1,0:T(8,128)S(1)}, f32[2,1024,128]{2,1,0:T(8,128)S(1)}, s32[1024,128]{1,0:T(8,128)S(1)}, f32[2,3,8,128]{3,2,1,0:T(8,128)S(1)}) custom-call(f32[768,128]{1,0:T(8,128)S(1)} %copy-done), custom_call_target="tpu_custom_call" | custom-call | tf_op jit(solution)/shard_map/own_first/pallas_call | solution.py:692
  10.7 0.0 collective-permute-done.from_down
  10.7 0.9 %collective-permute-done.1.from_up = f32[20,8,128]{2,1,0:T(8,128)S(1)} collective-permute-done((f32[20,8,128]{2,1,0:T(8,128)}, f32[20,8,128]{2,1,0:T(8,128)S(1)}, u32[]{:S(2)}, u32[]{:S(2)}) %collective-permute-start.1) | collective-permute-done | bytes 81952 | tf_op jit(solution)/shard_map/ppermute | solution.py:677
  11.6 0.1 pack_x.1
  11.7 0.0 copy-start.1
  11.7 0.0 copy-start.2
  11.7 2.3 %collective-permute-start.2 = (f32[21,24,128]{2,1,0:T(8,128)S(1)}, f32[21,24,128]{2,1,0:T(8,128)S(1)}, u32[]{:S(2)}, u32[]{:S(2)}) collective-permute-start(f32[21,24,128]{2,1,0:T(8,128)S(1)} %get-tuple-element.28), channel_id=1, source_target_pairs={{0,4},{4,8},{8,12},{12,16},{16,20},{20,24},{24,28},{28,0},{1,5},{5... | collective-permute-start | bytes 774152 | tf_op jit(solution)/shard_map/ppermute | solution.py:677
  14.0 0.0 collective-permute-start.3
  14.0 0.9 %own_second.1 = (f32[10,3,24,128]{3,2,1,0:T(8,128)S(1)}, f32[8,8,128]{2,1,0:T(8,128)S(1)}, f32[8,3,8,128]{3,2,1,0:T(8,128)S(1)}) custom-call(f32[768,128]{1,0:T(8,128)S(1)} %copy-done, f32[8,8,128]{2,1,0:T(8,128)S(1)} %get-tuple-element.19.part, f32[2,1024,128]{2,1,0:T(8,128)S(1)} %get-tuple-element.20.gb, s32[1024,128]{1,0:T(8,128)S(1)} %get-tuple-element.21.gz, ...), custom_call_target="tpu_custom_call" | custom-call | tf_op jit(solution)/shard_map/own_second/pallas_call | solution.py:692
  14.9 3.3 %collective-permute-done.2.from_left = f32[21,24,128]{2,1,0:T(8,128)S(1)} collective-permute-done((f32[21,24,128]{2,1,0:T(8,128)S(1)}, f32[21,24,128]{2,1,0:T(8,128)S(1)}, u32[]{:S(2)}, u32[]{:S(2)}) %collective-permute-start.2) | collective-permute-done | bytes 258080 | tf_op jit(solution)/shard_map/ppermute | solution.py:677
  18.2 3.5 %collective-permute-done.3.from_right = f32[21,24,128]{2,1,0:T(8,128)S(1)} collective-permute-done((f32[21,24,128]{2,1,0:T(8,128)S(1)}, f32[21,24,128]{2,1,0:T(8,128)S(1)}, u32[]{:S(2)}, u32[]{:S(2)}) %collective-permute-start.3) | collective-permute-done | bytes 258080 | tf_op jit(solution)/shard_map/ppermute | solution.py:677
  21.7 0.0 copy-done.1
  21.7 0.0 copy-done.2
  21.7 4.3 %main.1 = (f32[19,8,16,128]{3,2,1,0:T(8,128)}, f32[24,128]{1,0:T(8,128)}) custom-call(f32[19,8,16,128]{3,2,1,0:T(8,128)S(1)} %copy-done.2, f32[768,128]{1,0:T(8,128)S(1)} %copy-done.1, f32[2,8,8,128]{3,2,1,0:T(8,128)S(1)} %get-tuple-element.18.sides, f32[8,8,128]{2,1,0:T(8,128)S(1)} %get-tuple-element.25.react_in, ...), custom_call_target="tpu_custom_call" | custom-call | tf_op jit(solution)/shard_map/main/pallas_call | solution.py:692
Async XLA Ops:
  3.8 7.0 %collective-permute-start = (f32[20,8,128]{2,1,0:T(8,128)}, f32[20,8,128]{2,1,0:T(8,128)S(1)}, u32[]{:S(2)}, u32[]{:S(2)}) collective-permute-start(f32[20,8,128]{2,1,0:T(8,128)} %get-tuple-element.23), channel_id=1, source_target_pairs={{0,1},{1,2},{2,3},{3,0},{4,5},{5,6},{6,7},{7,4},{8,9},{9,10},{10,1... | collective-permute-start | bytes 245768 | tf_op jit(solution)/shard_map/ppermute | solution.py:677
  5.9 5.7 %collective-permute-start.1 = (f32[20,8,128]{2,1,0:T(8,128)}, f32[20,8,128]{2,1,0:T(8,128)S(1)}, u32[]{:S(2)}, u32[]{:S(2)}) collective-permute-start(f32[20,8,128]{2,1,0:T(8,128)} %get-tuple-element.24), channel_id=1, source_target_pairs={{0,3},{1,0},{2,1},{3,2},{4,7},{5,4},{6,5},{7,6},{8,11},{9,8},{10,9... | collective-permute-start | bytes 245768 | tf_op jit(solution)/shard_map/ppermute | solution.py:677
  8.0 1.0 %copy-start = (f32[768,128]{1,0:T(8,128)S(1)}, f32[768,128]{1,0:T(8,128)}, u32[]{:S(2)}) copy-start(f32[768,128]{1,0:T(8,128)} %get-tuple-element.17.mix) | copy-start | bytes 1179652
  11.7 10.0 %copy-start.1 = (f32[768,128]{1,0:T(8,128)S(1)}, f32[768,128]{1,0:T(8,128)}, u32[]{:S(2)}) copy-start(f32[768,128]{1,0:T(8,128)} %get-tuple-element.17.mix) | copy-start | bytes 1179652
  11.7 10.0 %copy-start.2 = (f32[19,8,16,128]{3,2,1,0:T(8,128)S(1)}, f32[19,8,16,128]{3,2,1,0:T(8,128)}, u32[]{:S(2)}) copy-start(f32[19,8,16,128]{3,2,1,0:T(8,128)} %pops.1) | copy-start | bytes 3735556
  11.7 6.5 %collective-permute-start.2 = (f32[21,24,128]{2,1,0:T(8,128)S(1)}, f32[21,24,128]{2,1,0:T(8,128)S(1)}, u32[]{:S(2)}, u32[]{:S(2)}) collective-permute-start(f32[21,24,128]{2,1,0:T(8,128)S(1)} %get-tuple-element.28), channel_id=1, source_target_pairs={{0,4},{4,8},{8,12},{12,16},{16,20},{20,24},{24,28},{28,0},{1,5},{5... | collective-permute-start | bytes 774152 | tf_op jit(solution)/shard_map/ppermute | solution.py:677
  14.0 7.7 %collective-permute-start.3 = (f32[21,24,128]{2,1,0:T(8,128)S(1)}, f32[21,24,128]{2,1,0:T(8,128)S(1)}, u32[]{:S(2)}, u32[]{:S(2)}) collective-permute-start(f32[21,24,128]{2,1,0:T(8,128)S(1)} %get-tuple-element.29), channel_id=1, source_target_pairs={{0,28},{4,0},{8,4},{12,8},{16,12},{20,16},{24,20},{28,24},{1,29},{... | collective-permute-start | bytes 774152 | tf_op jit(solution)/shard_map/ppermute | solution.py:677
